TPU v7x, 256 devices: a whole 4x4x8 slice. The times are simulated.
256 devices in a mesh: dp: 64 (over x_lo, y, z), seq: 4 (over x_hi, core).
Axes of the slice: x: 4 (x_hi: 2, x_lo: 2; x = x_hi * 2 + x_lo), y: 4, z: 8, core: 2. Of those that a mesh axis runs over, the one named last changes fastest.
Arguments:
- video_q: bfloat16 [32768, 1536], P(('dp', 'seq')), may hold values from -6 to 6
- video_k: bfloat16 [32768, 1536], P(('dp', 'seq')), may hold values from -6 to 6
- video_v: bfloat16 [32768, 1536], P(('dp', 'seq')), may hold values from -6 to 6
- text_q: bfloat16 [16384, 1536], P('dp'), may hold values from -6 to 6
- text_k: bfloat16 [16384, 1536], P('dp'), may hold values from -6 to 6
- text_v: bfloat16 [16384, 1536], P('dp'), may hold values from -6 to 6
- q_gain: float32 [128], replicated, may hold values from 0.5 to 1.5
- k_gain: float32 [128], replicated, may hold values from 0.5 to 1.5
- gate: bfloat16 [64, 3072], P('dp'), may hold values from -4 to 4
- out_weight: bfloat16 [1536, 3072], P(None, ('dp', 'seq')), may hold values from -0.15625 to 0.15625
- grad_out: bfloat16 [32768, 3072], P(('dp', 'seq')), may hold values from -24 to 24
- text_grad_out: bfloat16 [16384, 3072], P('dp'), may hold values from -6 to 6
Outputs:
- video_dq: bfloat16 [32768, 1536], P(('dp', 'seq'))
- video_dk: bfloat16 [32768, 1536], P(('dp', 'seq'))
- video_dv: bfloat16 [32768, 1536], P(('dp', 'seq'))
- text_dq: bfloat16 [16384, 1536], P('dp')
- text_dk: bfloat16 [16384, 1536], P('dp')
- text_dv: bfloat16 [16384, 1536], P('dp')
- weight_grad: float32 [1536, 3072], P('seq', 'dp')
- q_gain_grad: float32 [128], replicated
- k_gain_grad: float32 [128], replicated
All inputs are finite; a program needn't handle non-finite values.
Results may differ from a plain program's by a relative error of at most 0.012.
Values may be sent and summed in bfloat16 or wider, within the bound.
A program may use at most 128 MiB of HBM per device.

v0:
```python
import jax
import jax.numpy as jnp
from jax import lax
from jax.sharding import PartitionSpec as P


def head_grads(q, k, v, dout, q_gain, k_gain):
    scale = q.shape[-1] ** (-0.5)
    qf = q.astype(jnp.float32)
    kf = k.astype(jnp.float32)
    rq = lax.rsqrt(jnp.mean(qf * qf, axis=-1, keepdims=True) + 1e-06)
    rk = lax.rsqrt(jnp.mean(kf * kf, axis=-1, keepdims=True) + 1e-06)
    qn = (qf * rq * q_gain).astype(jnp.bfloat16)
    kn = (kf * rk * k_gain).astype(jnp.bfloat16)
    scores = (
        lax.dot_general(qn, kn, (((1,), (1,)), ((), ())), preferred_element_type=jnp.float32)
        * scale
    )
    expo = jnp.exp(scores)
    probs = expo / jnp.sum(expo, axis=-1, keepdims=True)
    probs_b = probs.astype(jnp.bfloat16)
    attn = jnp.dot(probs_b, v, preferred_element_type=jnp.float32).astype(jnp.bfloat16)
    grad_v = lax.dot_general(
        probs_b, dout, (((0,), (0,)), ((), ())), preferred_element_type=jnp.float32
    ).astype(jnp.bfloat16)
    grad_p = lax.dot_general(dout, v, (((1,), (1,)), ((), ())), preferred_element_type=jnp.float32)
    delta = jnp.sum(probs * grad_p, axis=-1, keepdims=True)
    grad_s = (probs * (grad_p - delta)).astype(jnp.bfloat16)
    grad_qn = jnp.dot(grad_s, kn, preferred_element_type=jnp.float32) * scale
    grad_kn = (
        lax.dot_general(grad_s, qn, (((0,), (0,)), ((), ())), preferred_element_type=jnp.float32)
        * scale
    )
    upper_q = grad_qn * q_gain
    upper_k = grad_kn * k_gain
    grad_q = rq * upper_q - qf * rq**3 * jnp.mean(upper_q * qf, axis=-1, keepdims=True)
    grad_k = rk * upper_k - kf * rk**3 * jnp.mean(upper_k * kf, axis=-1, keepdims=True)
    gain_q = jnp.sum(grad_qn * qf * rq, axis=0)
    gain_k = jnp.sum(grad_kn * kf * rk, axis=0)
    return (grad_q.astype(jnp.bfloat16), grad_k.astype(jnp.bfloat16), grad_v, attn, gain_q, gain_k)


def times_rows(left, rows):
    return lax.dot_general(
        left, rows, (((1,), (1,)), ((), ())), preferred_element_type=jnp.float32
    ).astype(jnp.bfloat16)


def shards(
    video_q,
    video_k,
    video_v,
    text_q,
    text_k,
    text_v,
    q_gain,
    k_gain,
    gate,
    out_weight,
    grad_out,
    text_grad_out,
):
    n_seq = lax.axis_size("seq")
    my_group = lax.axis_index("seq")
    head_size = q_gain.shape[0]
    own_cols = video_q.shape[1] // n_seq
    per_device = own_cols // head_size
    gate_f = gate.astype(jnp.float32)
    dyl = (grad_out.astype(jnp.float32) * gate_f).astype(jnp.bfloat16)
    tdyl = (text_grad_out.astype(jnp.float32) * gate_f).astype(jnp.bfloat16)
    dyl_clip = lax.all_gather(dyl, "seq", axis=0, tiled=True)
    full_weight = lax.all_gather(out_weight, ("dp", "seq"), axis=1, tiled=True)
    dout_tok = times_rows(dyl, full_weight)
    own_weight = lax.dynamic_slice_in_dim(full_weight, my_group * own_cols, own_cols, 0)
    vq, vk, vv, vdo = (
        lax.all_to_all(video_q, "seq", split_axis=1, concat_axis=0, tiled=True),
        lax.all_to_all(video_k, "seq", split_axis=1, concat_axis=0, tiled=True),
        lax.all_to_all(video_v, "seq", split_axis=1, concat_axis=0, tiled=True),
        lax.all_to_all(dout_tok, "seq", split_axis=1, concat_axis=0, tiled=True),
    )
    tdo = times_rows(tdyl, own_weight)
    start = my_group * own_cols
    tq = lax.dynamic_slice_in_dim(text_q, start, own_cols, 1)
    tk = lax.dynamic_slice_in_dim(text_k, start, own_cols, 1)
    tv = lax.dynamic_slice_in_dim(text_v, start, own_cols, 1)
    video_len = vq.shape[0]
    total = video_len + tq.shape[0]

    def split_heads(x):
        return x.reshape(total, per_device, head_size).transpose(1, 0, 2)

    def join_heads(x):
        return x.transpose(1, 0, 2).reshape(total, own_cols)

    q_all = jnp.concatenate([vq, tq], axis=0)
    k_all = jnp.concatenate([vk, tk], axis=0)
    v_all = jnp.concatenate([vv, tv], axis=0)
    d_all = jnp.concatenate([vdo, tdo], axis=0)
    results = lax.map(
        lambda a: head_grads(a[0], a[1], a[2], a[3], q_gain, k_gain),
        (split_heads(q_all), split_heads(k_all), split_heads(v_all), split_heads(d_all)),
    )
    grad_q = join_heads(results[0])
    grad_k = join_heads(results[1])
    grad_v = join_heads(results[2])
    attn = join_heads(results[3])
    dyl_all = jnp.concatenate([dyl_clip, tdyl], axis=0)
    term = lax.dot_general(
        attn, dyl_all, (((0,), (0,)), ((), ())), preferred_element_type=jnp.float32
    )
    weight_grad = lax.psum_scatter(term, "dp", scatter_dimension=1, tiled=True)
    q_gain_grad, k_gain_grad = lax.psum(
        (jnp.sum(results[4], axis=0), jnp.sum(results[5], axis=0)), ("dp", "seq")
    )
    video_dq, video_dk, video_dv = (
        lax.all_to_all(grad_q[:video_len], "seq", split_axis=0, concat_axis=1, tiled=True),
        lax.all_to_all(grad_k[:video_len], "seq", split_axis=0, concat_axis=1, tiled=True),
        lax.all_to_all(grad_v[:video_len], "seq", split_axis=0, concat_axis=1, tiled=True),
    )
    text_dq, text_dk, text_dv = (
        lax.all_gather(grad_q[video_len:], "seq", axis=1, tiled=True),
        lax.all_gather(grad_k[video_len:], "seq", axis=1, tiled=True),
        lax.all_gather(grad_v[video_len:], "seq", axis=1, tiled=True),
    )
    return (
        video_dq,
        video_dk,
        video_dv,
        text_dq,
        text_dk,
        text_dv,
        weight_grad,
        q_gain_grad,
        k_gain_grad,
    )


def solution(mesh):
    in_specs = (
        P(("dp", "seq"), None),
        P(("dp", "seq"), None),
        P(("dp", "seq"), None),
        P("dp", None),
        P("dp", None),
        P("dp", None),
        P(),
        P(),
        P("dp", None),
        P(None, ("dp", "seq")),
        P(("dp", "seq"), None),
        P("dp", None),
    )
    out_specs = (
        P(("dp", "seq"), None),
        P(("dp", "seq"), None),
        P(("dp", "seq"), None),
        P("dp", None),
        P("dp", None),
        P("dp", None),
        P("seq", "dp"),
        P(),
        P(),
    )
    return jax.shard_map(shards, mesh=mesh, in_specs=in_specs, out_specs=out_specs, check_vma=False)
```

profile of v0, /device:TPU:4, one launch (start us, length us, event | category | flops | bytes accessed | tf_op | source)
XLA Modules:
  0.0 855.8 jit_solution(15364594026396212774)
XLA Ops:
  7.9 1.9 copy.72
  9.9 5.8 all-to-all-start.1
  16.4 2.2 multiply_convert_fusion.2
  19.5 1.9 all-to-all-done.1
  21.4 6.7 all-to-all-start.3
  28.2 1.5 multiply_convert_fusion.1
  31.5 1.1 constant_dynamic-slice_fusion.2
  33.3 1.5 all-to-all-done.3
  34.8 6.5 all-to-all-start
  42.6 398.3 %all-gather.6.cloned.1.call-done = bf16[256,12,1536]{2,1,0:T(8,128)(2,1)} async-done(((bf16[1,12,1536]{2,1,0:T(8,128)(2,1)}), bf16[256,12,1536]{2,1,0:T(8,128)(2,1)}) %all-gather.6.cloned.1.call-update) | async-done | bytes 9437200 | tf_op jit(solution)/shard_map/all_gather | solution.py:72
  440.9 15.0 %reshape.147 = bf16[3072,1536]{1,0:T(8,128)(2,1)} reshape(bf16[256,12,1536]{2,1,0:T(8,128)(2,1)} %all-gather.6.cloned.1.call-done) | data formatting | bytes 18874368
  456.0 5.4 convolution_convert_fusion.2
  462.3 4.8 all-to-all-start.2
  468.4 2.7 fusion.77
  471.3 5.7 all-to-all-done.2
  477.5 1.1 maximum_bitcast_fusion
  478.6 38.9 %while.20 = (s32[]{:T(128)}, bf16[3,768,128]{1,2,0:T(8,128)(2,1)}, bf16[3,768,128]{1,2,0:T(8,128)(2,1)}, bf16[3,768,128]{1,2,0:T(8,128)(2,1)}, bf16[3,768,128]{1...) while((s32[]{:T(128)}, bf16[3,768,128]{1,2,0:T(8,128)(2,1)}, ...), condition=%wide.region_9.10_spmd, body=%wide.region_0.9_spmd.sunk | while | flops 921308160 | bytes 29996212 | solution.py:99
  478.6 0.9 constant_dynamic-slice_fusion.7
  479.9 0.9 constant_dynamic-slice_fusion.8
  482.0 1.5 fusion.117
  483.6 1.5 fusion.116
  486.0 1.7 multiply_reduce_fusion.2
  491.6 0.9 constant_dynamic-slice_fusion.7
  492.9 0.9 constant_dynamic-slice_fusion.8
  494.9 1.5 fusion.117
  496.6 1.5 fusion.116
  499.0 1.7 multiply_reduce_fusion.2
  504.6 0.9 constant_dynamic-slice_fusion.7
  505.9 0.9 constant_dynamic-slice_fusion.8
  507.9 1.5 fusion.117
  509.5 1.5 fusion.116
  512.0 1.7 multiply_reduce_fusion.2
  517.6 7.3 fusion.71
  524.9 1.0 copy-done.8
  527.3 7.0 all-to-all-start.4
  536.1 10.2 %all_gather.18 = bf16[256,1536]{0,1:T(8,128)(2,1)S(1)} all-gather(bf16[256,384]{0,1:T(8,128)(2,1)S(1)} %bitcast.227), channel_id=1, replica_groups=mesh['dp'=64,'seq'=4] {'seq'}, dimensions={1}, use_global_device_ids=true | all-gather | bytes 983040 | tf_op jit(solution)/shard_map/all_gather | solution.py:123
  546.3 1.2 copy.97
  547.5 5.4 all-to-all-start.5
  552.9 10.9 %all_gather.17 = bf16[256,1536]{0,1:T(8,128)(2,1)S(1)} all-gather(bf16[256,384]{0,1:T(8,128)(2,1)S(1)} %bitcast.226), channel_id=1, replica_groups=mesh['dp'=64,'seq'=4] {'seq'}, dimensions={1}, use_global_device_ids=true | all-gather | bytes 983040 | tf_op jit(solution)/shard_map/all_gather | solution.py:122
  563.8 1.2 copy.96
  564.9 6.6 all-to-all-start.6
  571.5 10.9 %all_gather.16 = bf16[256,1536]{0,1:T(8,128)(2,1)S(1)} all-gather(bf16[256,384]{0,1:T(8,128)(2,1)S(1)} %bitcast.225), channel_id=1, replica_groups=mesh['dp'=64,'seq'=4] {'seq'}, dimensions={1}, use_global_device_ids=true | all-gather | bytes 983040 | tf_op jit(solution)/shard_map/all_gather | solution.py:121
  582.4 1.2 copy.95
  583.6 81.3 %all-reduce = (f32[128]{0:T(128)}, f32[128]{0:T(128)}) all-reduce(f32[128]{0:T(128)S(1)} %reduce_sum.90, f32[128]{0:T(128)S(1)} %reduce_sum.91), channel_id=1, replica_groups=mesh['dp'=64,'seq'=4] {'dp','seq'}, use_global_device_ids=true, to_apply=%region_12.13 | all-reduce | flops 256 | bytes 2048 | tf_op jit(solution)/shard_map/psum | solution.py:112
  664.9 0.9 copy.92
  665.8 0.9 copy.93
  666.7 0.9 copy.94
  667.7 181.6 %reduce-scatter.2.cloned.1.call-done = f32[384,48]{0,1:T(8,128)} async-done(((f32[384,3072]{0,1:T(8,128)}), f32[384,48]{0,1:T(8,128)}) %reduce-scatter.2.cloned.1.call-update) | async-done | bytes 73744 | tf_op jit(solution)/shard_map/reduce_scatter | solution.py:111
  (147 shorter events, 31.3 us)
Async XLA Ops:
  7.2 22.5 %copy-start = (bf16[256,1536]{1,0:T(8,128)(2,1)S(1)}, bf16[256,1536]{1,0:T(8,128)(2,1)}, u32[]{:S(2)}) copy-start(bf16[256,1536]{1,0:T(8,128)(2,1)} %param.17) | copy-start | bytes 2359300
  7.2 11.4 %copy-start.9 = (bf16[128,1536]{1,0:T(8,128)(2,1)S(1)}, bf16[128,1536]{1,0:T(8,128)(2,1)}, u32[]{:S(2)}) copy-start(bf16[128,1536]{1,0:T(8,128)(2,1)} %param.16) | copy-start | bytes 1179652
  7.2 433.7 %all-gather.6.cloned.1.call-start = ((), (), s32[]{:S(2)}) async-start(), calls=%async_computation.10 | async-start | bytes 12632064 | tf_op jit(solution)/shard_map/all_gather | solution.py:72
  9.9 18.3 %copy-start.3 = (bf16[256,3072]{1,0:T(8,128)(2,1)S(1)}, bf16[256,3072]{1,0:T(8,128)(2,1)}, u32[]{:S(2)}) copy-start(bf16[256,3072]{1,0:T(8,128)(2,1)} %param.25) | copy-start | bytes 4718596
  9.9 11.6 %all-to-all-start.1 = ((bf16[128,4,384]{0,2,1:T(8,128)(2,1)}), bf16[128,4,384]{0,2,1:T(8,128)(2,1)S(1)}, u32[]{:S(2)}, u32[]{:S(2)}) async-start(bf16[128,4,384]{0,2,1:T(8,128)(2,1)} %bitcast.16), calls=%async_computation.1 | async-start | bytes 786432 | tf_op jit(solution)/shard_map/all_to_all | solution.py:77
  15.7 501.9 %all-gather.4.cloned.1.call-start = ((), (), s32[]{:S(2)}) async-start(), calls=%async_computation.8 | async-start | bytes 3932160 | tf_op jit(solution)/shard_map/all_gather | solution.py:71
  21.4 9.1 %copy-start.10 = (bf16[128,1536]{1,0:T(8,128)(2,1)S(1)}, bf16[128,1536]{1,0:T(8,128)(2,1)}, u32[]{:S(2)}) copy-start(bf16[128,1536]{1,0:T(8,128)(2,1)} %param.14) | copy-start | bytes 1179652
  21.4 13.4 %all-to-all-start.3 = ((bf16[128,4,384]{0,2,1:T(8,128)(2,1)}), bf16[128,4,384]{0,2,1:T(8,128)(2,1)S(1)}, u32[]{:S(2)}, u32[]{:S(2)}) async-start(bf16[128,4,384]{0,2,1:T(8,128)(2,1)} %bitcast.27), calls=%async_computation.3 | async-start | bytes 786432 | tf_op jit(solution)/shard_map/all_to_all | solution.py:78
  34.8 427.5 %all-to-all-start = ((bf16[128,4,384]{0,2,1:T(8,128)(2,1)}), bf16[128,4,384]{0,2,1:T(8,128)(2,1)S(1)}, u32[]{:S(2)}, u32[]{:S(2)}) async-start(bf16[128,4,384]{0,2,1:T(8,128)(2,1)} %bitcast.12), calls=%async_computation | async-start | bytes 786432 | tf_op jit(solution)/shard_map/all_to_all | solution.py:76
  42.6 413.3 %copy-start.2 = (bf16[128,3072]{1,0:T(8,128)(2,1)S(1)}, bf16[128,3072]{1,0:T(8,128)(2,1)}, u32[]{:S(2)}) copy-start(bf16[128,3072]{1,0:T(8,128)(2,1)} %multiply_convert_fusion.2) | copy-start | bytes 2359300
  461.3 7.1 copy-start.4
  462.3 14.8 %all-to-all-start.2 = ((bf16[128,4,384]{0,2,1:T(8,128)(2,1)}), bf16[128,4,384]{0,2,1:T(8,128)(2,1)S(1)}, u32[]{:S(2)}, u32[]{:S(2)}) async-start(bf16[128,4,384]{0,2,1:T(8,128)(2,1)} %bitcast.23), calls=%async_computation.2 | async-start | bytes 786432 | tf_op jit(solution)/shard_map/all_to_all | solution.py:79
  467.1 382.2 %reduce-scatter.2.cloned.1.call-start = ((), (), s32[]{:S(2)}) async-start(), calls=%async_computation.9 | async-start | bytes 4792320 | tf_op jit(solution)/shard_map/reduce_scatter | solution.py:111
  468.4 9.1 %copy-start.5 = (bf16[256,384]{0,1:T(8,128)(2,1)S(1)}, bf16[256,384]{0,1:T(8,128)(2,1)}, u32[]{:S(2)}) copy-start(bf16[256,384]{0,1:T(8,128)(2,1)} %copy.111) | copy-start | bytes 589828
  471.1 7.5 copy-start.11
  471.1 7.5 copy-start.12
  524.9 1.1 copy-start.8
  524.9 1.2 copy-start.7
  524.9 1.4 copy-start.6
  527.3 20.2 %all-to-all-start.4 = ((bf16[4,128,384]{1,2,0:T(8,128)(2,1)}), bf16[4,128,384]{1,2,0:T(8,128)(2,1)S(1)}, u32[]{:S(2)}, u32[]{:S(2)}) async-start(bf16[4,128,384]{1,2,0:T(8,128)(2,1)} %copy.86), calls=%async_computation.4 | async-start | bytes 786432 | tf_op jit(solution)/shard_map/all_to_all | solution.py:116
  547.5 17.5 %all-to-all-start.5 = ((bf16[4,128,384]{1,2,0:T(8,128)(2,1)}), bf16[4,128,384]{1,2,0:T(8,128)(2,1)S(1)}, u32[]{:S(2)}, u32[]{:S(2)}) async-start(bf16[4,128,384]{1,2,0:T(8,128)(2,1)} %copy.88), calls=%async_computation.5 | async-start | bytes 786432 | tf_op jit(solution)/shard_map/all_to_all | solution.py:117
  564.9 101.8 %all-to-all-start.6 = ((bf16[4,128,384]{1,2,0:T(8,128)(2,1)}), bf16[4,128,384]{1,2,0:T(8,128)(2,1)S(1)}, u32[]{:S(2)}, u32[]{:S(2)}) async-start(bf16[4,128,384]{1,2,0:T(8,128)(2,1)} %copy.90), calls=%async_computation.6 | async-start | bytes 786432 | tf_op jit(solution)/shard_map/all_to_all | solution.py:118
  571.5 277.7 %copy-start.1 = (bf16[256,1536]{1,0:T(8,128)(2,1)S(1)}, bf16[256,1536]{1,0:T(8,128)(2,1)}, u32[]{:S(2)}) copy-start(bf16[256,1536]{1,0:T(8,128)(2,1)} %param.17) | copy-start | bytes 2359300
Sparse Core Ops, SparseCore 0:
  9.9 430.9 all-gather.5
  443.3 35.9 all-gather.3
  525.1 324.1 reduce-scatter.1
where the time goes:
time: 857 us; the launch traced here: 856 us
  waiting for transfers between devices  590 us (69%)
  blocking collectives  113 us (13%)
  local copies, waits for them, and re-layouts  47.6 us (6%)
  starting transfers between devices  42.8 us (5%)
  matrix products  35.7 us (4%)
  between operations  14 us (2%)
  other arithmetic  12.3 us (1%)
    all_gather x1, waiting for transfers between devices, shards(): full_weight = lax.all_gather(out_weight, ('dp', 'seq'), axis=1, tiled=True)  398 us
    reduce_scatter x1, waiting for transfers between devices, shards(): weight_grad = lax.psum_scatter(term, 'dp', scatter_dimension=1, tiled=True)  182 us
    psum x1, blocking collectives, shards(): lax.psum((jnp.sum(results[4], axis=0), jnp.sum(results[5], axis=0)), ('dp...  81.3 us
    unnamed x39, local copies, waits for them, and re-layouts  27.5 us
  transfers between devices with their start and end apart: 10, of which 5 were waited for; matrix products, arithmetic and copies ran while one was open for 10% of the time, Pallas kernels for 0%

commit v1 on v0

v1 whole, which is shorter than its diff:
```python
import functools

import jax
import jax.numpy as jnp
from jax import lax
from jax.experimental import pallas as pl
from jax.experimental.pallas import tpu as pltpu
from jax.sharding import PartitionSpec as P

MESH = pl.DeviceIdType.MESH
BF, F32 = jnp.bfloat16, jnp.float32

XL, NY, NZ, NS = 2, 4, 8, 4
HD = 128
G = 3
GC = G * HD
V = 128
VID, TXT = 512, 256
TOK = VID + TXT
D = 3072
WCOL = 12
WB = 48
QC = 256
PIECES = 8
SCALE = HD**-0.5
LOG2E = 1.4426950408889634


def dot(a, b, ca=1, cb=0):
    return lax.dot_general(a, b, (((ca,), (cb,)), ((), ())), preferred_element_type=F32)


def kernel(
    vq, vk, vv, tq, tk, tv, qg, kg, gate, wt, go, tgo,
    o_video, o_text, o_w, o_gain,
    qb, kb, vb, dyr, dyb, wbuf, wslot, w48, dout, grads,
    qn_s, kn_s, knt_s, vt_s, ot_s, dk_a, dv_a, gains,
    tbuf, rbuf, zs, zr, xsum, xr, g_seq, g_x, g_y, g_z,
    ssem, rsem, lsem,
):
    dp, s = lax.axis_index("dp"), lax.axis_index("seq")
    xl, y, z = dp // (NY * NZ), (dp // NZ) % NY, dp % NZ
    core = s + 1 - 2 * (s % 2)
    part = (s + 2) % NS
    diag = (core + 2) % NS
    seq_peer = {1: core, 2: part, 3: diag}

    def ydev(k):
        return (xl * (NY * NZ) + ((y + NY + k) % NY) * NZ + z, s)

    def zdev(k):
        return (xl * (NY * NZ) + y * NZ + (z + NZ + k) % NZ, s)

    xdev = ((dp + NY * NZ) % (XL * NY * NZ), s)

    def sdev(d):
        return (dp, seq_peer[d])

    names = {}
    pending = []
    local = []

    def remote(key, src, dst, dev):
        i = names.setdefault(key, len(names))
        return pltpu.make_async_remote_copy(
            src_ref=src, dst_ref=dst, send_sem=ssem.at[i], recv_sem=rsem.at[i],
            device_id=dev, device_id_type=MESH,
        )

    def send(key, src, dst, dev):
        copy = remote(key, src, dst, dev)
        copy.start()
        pending.append(copy)

    def arrived(key, dst, dev):
        remote(key, dst, dst, dev).wait_recv()

    def here(src, dst):
        copy = pltpu.make_async_copy(src, dst, lsem.at[len(local)])
        copy.start()
        local.append(copy)
        return copy

    def rows_of(j):
        return pl.ds(pl.multiple_of(j * V, V), V)

    def cols_of(j):
        return pl.ds(pl.multiple_of(j * GC, GC), GC)

    def head_cols(j, h):
        return pl.ds(pl.multiple_of(j * GC + h * HD, HD), HD)

    peers = [sdev(1), sdev(2), sdev(3), xdev] + [ydev(k) for k in range(1, NY)] + [zdev(k) for k in range(1, NZ)]
    barrier = pltpu.get_barrier_semaphore()
    for dev in peers:
        pl.semaphore_signal(barrier, inc=1, device_id=dev, device_id_type=MESH)

    own_w = here(wt.at[:, cols_of(s)], wslot.at[s])
    own_dy = here(go, dyr.at[rows_of(s)])
    text_dy = here(tgo, dyr.at[pl.ds(VID, TXT)])
    own = []
    for src, tsrc, dst in ((vq, tq, qb), (vk, tk, kb), (vv, tv, vb)):
        own.append(here(src.at[:, cols_of(s)], dst.at[rows_of(s)]))
        own.append(here(tsrc.at[:, cols_of(s)], dst.at[pl.ds(VID, TXT)]))
    pl.semaphore_wait(barrier, len(peers))

    for d in (1, 2, 3):
        send(("w", d), wt.at[:, cols_of(seq_peer[d])], wslot.at[s], sdev(d))
    piece = V // PIECES

    def dy_piece(j, t):
        return dyr.at[pl.ds(pl.multiple_of(j * V + t * piece, piece), piece)]

    for t in range(PIECES):
        send(("dyx", t), go.at[pl.ds(t * piece, piece)], dy_piece(s, t), sdev(2))
    send("dyc", go, dyr.at[rows_of(s)], sdev(1))
    for h in range(G):
        for d in (2, 3, 1):
            for n, (src, dst) in enumerate(((vq, qb), (vk, kb), (vv, vb))):
                send(("in", h, d, n), src.at[:, head_cols(seq_peer[d], h)],
                     dst.at[rows_of(s), pl.ds(h * HD, HD)], sdev(d))

    own_w.wait()
    for d in (1, 2, 3):
        arrived(("w", d), wslot.at[seq_peer[d]], sdev(d))
    for j in range(NS):
        w48[pl.ds(j * WCOL, WCOL), :] = wslot[j].astype(F32)[:WCOL]
    wbuf[xl, y, z] = w48[...].astype(BF)
    send("wx", wbuf.at[xl, y, z], wbuf.at[xl, y, z], xdev)
    arrived("wx", wbuf.at[1 - xl, y, z], xdev)

    ca, cb = pl.ds(HD, GC - HD), pl.ds(0, HD)

    def blk_a(ky, kz):
        return wbuf.at[:, (y + NY + ky) % NY, (z + NZ + kz) % NZ, :, ca]

    def blk_b(kz):
        return wbuf.at[:, :, (z + NZ + kz) % NZ, :, cb]

    def along_y(kz):
        for k in range(1, NY):
            send(("wya", kz % NZ, k), blk_a(0, kz), blk_a(0, kz), ydev(k))

    for k in range(1, NY):
        mine = wbuf.at[:, y, z, :, cb]
        send(("wyb", k), mine, mine, ydev(k))
    send(("wza+", 0), blk_a(0, 0), blk_a(0, 0), zdev(1))
    send(("wza-", 0), blk_a(0, 0), blk_a(0, 0), zdev(-1))
    along_y(0)
    for k in range(1, NY):
        arrived(("wyb", k), wbuf.at[:, (y + NY - k) % NY, z, :, cb], ydev(-k))
    send(("wzb+", 0), blk_b(0), blk_b(0), zdev(1))
    send(("wzb-", 0), blk_b(0), blk_b(0), zdev(-1))

    def pass_on_dy(t):
        arrived(("dyx", t), dy_piece(part, t), sdev(2))
        send(("dyr", t), dy_piece(part, t), dy_piece(part, t), sdev(1))

    gate_f = gate[...].astype(F32)

    def gated(j, count):
        def body(i, carry):
            at = pl.ds(pl.multiple_of(j * V + i * 32, 32), 32)
            dyb[at, :] = (dyr[at, :].astype(F32) * gate_f).astype(BF)
            return carry
        lax.fori_loop(0, count // 32, body, 0)

    last_p, last_m = NZ // 2, NZ // 2 - 1
    for t in range(last_p):
        arrived(("wza+", t), blk_a(0, -1 - t), zdev(-1))
        if t + 1 < last_p:
            send(("wza+", t + 1), blk_a(0, -1 - t), blk_a(0, -1 - t), zdev(1))
        along_y(-1 - t)
        if t < last_m:
            arrived(("wza-", t), blk_a(0, 1 + t), zdev(1))
            if t + 1 < last_m:
                send(("wza-", t + 1), blk_a(0, 1 + t), blk_a(0, 1 + t), zdev(-1))
            along_y(1 + t)
        arrived(("wzb+", t), blk_b(-1 - t), zdev(-1))
        if t + 1 < last_p:
            send(("wzb+", t + 1), blk_b(-1 - t), blk_b(-1 - t), zdev(1))
        if t < last_m:
            arrived(("wzb-", t), blk_b(1 + t), zdev(1))
            if t + 1 < last_m:
                send(("wzb-", t + 1), blk_b(1 + t), blk_b(1 + t), zdev(-1))
        pass_on_dy(t)
        if t == 0:
            own_dy.wait()
            gated(s, V)
        if t == 1:
            text_dy.wait()
            gated(NS, TXT)
        if t == 2:
            arrived("dyc", dyr.at[rows_of(core)], sdev(1))
            gated(core, V)
    for t in range(last_p, PIECES):
        pass_on_dy(t)
    gated(part, V)
    for kz in range(NZ):
        for k in range(1, NY):
            arrived(("wya", kz, k), blk_a(-k, kz), ydev(-k))
    for t in range(PIECES):
        arrived(("dyr", t), dy_piece(diag, t), sdev(1))
    gated(diag, V)

    def dout_rows(i, carry):
        at = pl.ds(pl.multiple_of(i * 128, 128), 128)
        w = wbuf[...].reshape(D, GC)
        dout[at, :] = dot(dyb[at, :], w).astype(BF)
        return carry
    lax.fori_loop(0, TOK // 128, dout_rows, 0)

    for copy in own:
        copy.wait()
    q_gain, k_gain = qg[...], kg[...]
    gains[...] = jnp.zeros_like(gains)

    def norm(x):
        return lax.rsqrt(jnp.sum(x * x, axis=-1, keepdims=True) * (1.0 / HD) + 1e-06)

    def through_norm(x, r, u):
        return r * u - x * (r * r * r) * (jnp.sum(u * x, axis=-1, keepdims=True) * (1.0 / HD))

    def head(h):
        cols = pl.ds(h * HD, HD)
        qf = qb[:, cols].astype(F32)
        qn_s[...] = (qf * norm(qf) * q_gain).astype(BF)
        kf = kb[:, cols].astype(F32)
        kn = kf * norm(kf) * k_gain
        kn_s[...] = kn.astype(BF)
        knt_s[...] = kn.T.astype(BF)
        vt_s[...] = vb[:, cols].astype(F32).T.astype(BF)
        dk_a[...] = jnp.zeros_like(dk_a)
        dv_a[...] = jnp.zeros_like(dv_a)

        def chunk(c, carry):
            at = pl.ds(pl.multiple_of(c * QC, QC), QC)
            qn, do = qn_s[at, :], dout[at, cols]
            e = jnp.exp2(dot(kn_s[...], qn, 1, 1) * (SCALE * LOG2E))
            p = e * (1.0 / jnp.sum(e, axis=0, keepdims=True))
            pb = p.astype(BF)
            dv_a[...] += dot(pb, do)
            ot_s[:, at] = dot(vt_s[...], pb).astype(BF)
            dpr = dot(vb[:, cols], do, 1, 1)
            delta = jnp.sum(p * dpr, axis=0, keepdims=True)
            ds = (p * (dpr - delta)).astype(BF)
            dk_a[...] += dot(ds, qn)
            dqn = dot(knt_s[...], ds).T * SCALE
            x = qb[at, cols].astype(F32)
            r = norm(x)
            grads[h, 0, at, :] = through_norm(x, r, dqn * q_gain).astype(BF)
            gains[0:1, :] += jnp.sum(dqn * x * r, axis=0, keepdims=True)
            return carry
        lax.fori_loop(0, TOK // QC, chunk, 0)
        dkn = dk_a[...] * SCALE
        x = kb[:, cols].astype(F32)
        r = norm(x)
        grads[h, 1] = through_norm(x, r, dkn * k_gain).astype(BF)
        gains[1:2, :] += jnp.sum(dkn * x * r, axis=0, keepdims=True)
        grads[h, 2] = dv_a[...].astype(BF)

    def term(h):
        def body(n, carry):
            at = pl.ds(pl.multiple_of(n * GC, GC), GC)
            tbuf[h, n // NY, n % NY] = dot(ot_s[...], dyb[:, at]).astype(BF)
            return carry
        lax.fori_loop(0, XL * NY, body, 0)

    text = pl.ds(VID, TXT)
    out_local = []
    for h in range(G):
        for d in (2, 3, 1):
            for n, dst in enumerate((qb, kb, vb)):
                arrived(("in", h, d, n), dst.at[rows_of(seq_peer[d]), pl.ds(h * HD, HD)], sdev(d))
        head(h)
        to = head_cols(s, h)
        send(("text", h, 2), grads.at[h, :, text], o_text.at[:, :, to], sdev(2))
        send(("text", h, 1), grads.at[h, :, text], o_text.at[:, :, to], sdev(1))
        for d in (2, 3, 1):
            send(("out", h, d), grads.at[h, :, rows_of(seq_peer[d])], o_video.at[:, :, to], sdev(d))
        out_local.append(here(grads.at[h, :, rows_of(s)], o_video.at[:, :, to]))
        out_local.append(here(grads.at[h, :, text], o_text.at[:, :, to]))
        term(h)
        for k in range(1, NY):
            send(("ty", h, k), tbuf.at[h, :, (y + k) % NY], rbuf.at[h, k - 1], ydev(k))

    g_seq[s] = gains[...]
    for d in (1, 2, 3):
        send(("gs", d), g_seq.at[s], g_seq.at[s], sdev(d))

    def pass_on_text(h):
        at = o_text.at[:, :, head_cols(part, h)]
        arrived(("text", h, 2), at, sdev(2))
        send(("textr", h), at, at, sdev(1))

    def y_sum(h):
        for k in range(1, NY):
            arrived(("ty", h, k), rbuf.at[h, k - 1], ydev(-k))
        for i in range(XL):
            total = tbuf[h, i, y].astype(F32)
            for k in range(1, NY):
                total += rbuf[h, k - 1, i].astype(F32)
            zs[h, :, i] = total.T.reshape(NZ, WB, HD).astype(BF)
        for k in range(1, NZ):
            send(("tz", h, k), zs.at[h, (z + k) % NZ], zr.at[h, k - 1], zdev(k))

    def z_sum(h):
        for k in range(1, NZ):
            arrived(("tz", h, k), zr.at[h, k - 1], zdev(-k))
        total = zs[h, z].astype(F32)
        for k in range(1, NZ):
            total += zr[h, k - 1].astype(F32)
        xsum[:, :, h * HD:(h + 1) * HD] = total

    y_sum(0)
    for d in (1, 2, 3):
        arrived(("gs", d), g_seq.at[seq_peer[d]], sdev(d))
    g_x[xl] = g_seq[0] + g_seq[1] + g_seq[2] + g_seq[3]
    send("gx", g_x.at[xl], g_x.at[xl], xdev)
    pass_on_text(0)
    y_sum(1)
    arrived("gx", g_x.at[1 - xl], xdev)
    g_y[y] = g_x[0] + g_x[1]
    for k in range(1, NY):
        send(("gy", k), g_y.at[y], g_y.at[y], ydev(k))
    z_sum(0)
    pass_on_text(1)
    y_sum(2)
    for k in range(1, NY):
        arrived(("gy", k), g_y.at[(y + NY - k) % NY], ydev(-k))
    g_z[z] = (g_y[0] + g_y[1]) + (g_y[2] + g_y[3])
    for k in range(1, NZ):
        send(("gz", k), g_z.at[z], g_z.at[z], zdev(k))
    z_sum(1)
    z_sum(2)
    send("tx", xsum.at[1 - xl], xr, xdev)
    for k in range(1, NZ):
        arrived(("gz", k), g_z.at[(z + NZ - k) % NZ], zdev(-k))
    total = g_z[0]
    for k in range(1, NZ):
        total += g_z[k]
    o_gain[...] = total
    arrived("tx", xr, xdev)
    o_w[...] = xsum[xl] + xr[...]
    pass_on_text(2)

    for h in range(G):
        arrived(("text", h, 1), o_text.at[:, :, head_cols(core, h)], sdev(1))
        arrived(("textr", h), o_text.at[:, :, head_cols(diag, h)], sdev(1))
        for d in (1, 2, 3):
            arrived(("out", h, d), o_video.at[:, :, head_cols(seq_peer[d], h)], sdev(d))
    for copy in out_local:
        copy.wait()
    for copy in pending:
        copy.wait_send()


def shards(video_q, video_k, video_v, text_q, text_k, text_v, q_gain, k_gain, gate, out_weight, grad_out, text_grad_out):
    wt = jnp.pad(out_weight.T, ((0, 16 - WCOL), (0, 0)))
    hbm = pl.BlockSpec(memory_space=pl.ANY)
    vmem = pl.BlockSpec(memory_space=pltpu.VMEM)
    video, text, w, gains = pl.pallas_call(
        kernel,
        out_shape=[
            jax.ShapeDtypeStruct((3, V, NS * GC), BF),
            jax.ShapeDtypeStruct((3, TXT, NS * GC), BF),
            jax.ShapeDtypeStruct((WB, GC), F32),
            jax.ShapeDtypeStruct((8, HD), F32),
        ],
        in_specs=[hbm] * 6 + [vmem] * 3 + [hbm] * 3,
        out_specs=[hbm, hbm, vmem, vmem],
        scratch_shapes=[
            pltpu.VMEM((TOK, GC), BF),
            pltpu.VMEM((TOK, GC), BF),
            pltpu.VMEM((TOK, GC), BF),
            pltpu.VMEM((TOK, D), BF),
            pltpu.VMEM((TOK, D), BF),
            pltpu.VMEM((XL, NY, NZ, WB, GC), BF),
            pltpu.VMEM((NS, 16, GC), BF),
            pltpu.VMEM((WB, GC), F32),
            pltpu.VMEM((TOK, GC), BF),
            pltpu.VMEM((G, 3, TOK, HD), BF),
            pltpu.VMEM((TOK, HD), BF),
            pltpu.VMEM((TOK, HD), BF),
            pltpu.VMEM((HD, TOK), BF),
            pltpu.VMEM((HD, TOK), BF),
            pltpu.VMEM((HD, TOK), BF),
            pltpu.VMEM((TOK, HD), F32),
            pltpu.VMEM((TOK, HD), F32),
            pltpu.VMEM((8, HD), F32),
            pltpu.VMEM((G, XL, NY, HD, GC), BF),
            pltpu.VMEM((G, NY - 1, XL, HD, GC), BF),
            pltpu.VMEM((G, NZ, XL, WB, HD), BF),
            pltpu.VMEM((G, NZ - 1, XL, WB, HD), BF),
            pltpu.VMEM((XL, WB, GC), F32),
            pltpu.VMEM((WB, GC), F32),
            pltpu.VMEM((NS, 8, HD), F32),
            pltpu.VMEM((XL, 8, HD), F32),
            pltpu.VMEM((NY, 8, HD), F32),
            pltpu.VMEM((NZ, 8, HD), F32),
            pltpu.SemaphoreType.DMA((160,)),
            pltpu.SemaphoreType.DMA((160,)),
            pltpu.SemaphoreType.DMA((16,)),
        ],
        compiler_params=pltpu.CompilerParams(
            collective_id=0, has_side_effects=True, vmem_limit_bytes=50 << 20
        ),
        cost_estimate=pl.CostEstimate(flops=7 * 10**9, bytes_accessed=14 << 20, transcendentals=1 << 21),
    )(
        video_q, video_k, video_v, text_q, text_k, text_v,
        q_gain.reshape(1, HD), k_gain.reshape(1, HD), gate, wt, grad_out, text_grad_out,
    )
    return (
        video[0], video[1], video[2], text[0], text[1], text[2],
        w.T, gains[0], gains[1],
    )


def solution(mesh):
    rows, clip = P(("dp", "seq"), None), P("dp", None)
    return jax.shard_map(
        shards,
        mesh=mesh,
        in_specs=(rows,) * 3 + (clip,) * 3 + (P(), P(), clip, P(None, ("dp", "seq")), rows, clip),
        out_specs=(rows,) * 3 + (clip,) * 3 + (P("seq", "dp"), P(), P()),
        check_vma=False,
    )
```

time: 857 us -> 138 us (0.16)
  the two profiles are of different devices: /device:TPU:4 before, /device:TPU:1 now
where the time goes in v1:
time: 138 us
  Pallas kernels  123 us (89%)
  local copies, waits for them, and re-layouts  14.2 us (10%)
    pallas_call x1, Pallas kernels, shards(): pl.pallas_call(kernel, out_shape=[jax.ShapeDtypeStruct((3, V, NS * GC), B...  123 us
    unnamed x21, local copies, waits for them, and re-layouts  9.03 us

profile of v1, /device:TPU:1, one launch (start us, length us, event | category | flops | bytes accessed | tf_op | source)
XLA Modules:
  0.0 137.5 jit_solution(7931735962526401143)
XLA Ops:
  0.6 0.8 pad.4.wt
  1.5 0.0 copy-start
  1.5 1.1 copy-done
  2.6 0.0 copy-start.1
  2.6 1.1 copy-done.1
  3.7 0.0 copy-start.2
  3.7 1.1 copy-done.2
  4.9 0.0 copy-start.3
  4.9 1.0 copy-done.3
  5.8 0.0 copy-start.4
  5.8 1.0 copy-done.4
  6.8 0.0 copy-start.5
  6.8 1.0 copy-done.5
  7.8 0.0 copy-start.6
  7.8 0.7 copy-done.6
  8.5 0.0 copy-start.7
  8.6 0.7 copy-done.7
  9.2 0.0 copy-start.8
  9.2 0.7 copy-done.8
  9.9 122.6 %shard_map.187 = (bf16[3,128,1536]{2,1,0:T(8,128)(2,1)}, bf16[3,256,1536]{2,1,0:T(8,128)(2,1)}, f32[48,384]{1,0:T(8,128)S(1)}, f32[8,128]{1,0:T(8,128)S(1)}) custom-call(bf16[128,1536]{1,0:T(8,128)(2,1)S(1)} %copy-done.3, bf16[128,1536]{1,0:T(8,128)(2,1)S(1)} %copy-done.4, bf16[128,1536]{1,0:T(8,128)(2,1)S(1)} %copy-done.5, bf16[256,1536]{1,0:T(8,128)(2,1)S(1)} %copy-done, ...), custom_call_target="tpu_custom_call" | custom-call | flops 7000000000 | bytes 14680064 | tf_op jit(solution)/shard_map/pallas_call | solution.py:362
  132.5 0.0 copy-start.9
  132.5 2.4 %slice_bitcast_fusion.3 = (bf16[128,1536]{1,0:T(8,128)(2,1)}, bf16[128,1536]{1,0:T(8,128)(2,1)}, bf16[128,1536]{1,0:T(8,128)(2,1)}) fusion(bf16[3,128,1536]{2,1,0:T(8,128)(2,1)} %get-tuple-element.13), kind=kLoop, calls=%fused_computation.3 | loop fusion | bytes 2359296 | tf_op jit(solution)/shard_map/squeeze | solution.py:414
  134.9 0.5 slice_bitcast_fusion.6
  135.4 0.0 copy-done.9
  135.4 1.4 %slice_bitcast_fusion = (bf16[256,1536]{1,0:T(8,128)(2,1)}, bf16[256,1536]{1,0:T(8,128)(2,1)}, bf16[256,1536]{1,0:T(8,128)(2,1)}) fusion(bf16[3,256,1536]{2,1,0:T(8,128)(2,1)S(1)} %copy-done.9), kind=kLoop, calls=%fused_computation | loop fusion | bytes 4718592 | tf_op jit(solution)/shard_map/squeeze | solution.py:414
  136.9 0.6 copy.22
Async XLA Ops:
  1.5 1.1 copy-start
  2.6 1.1 copy-start.1
  3.7 1.1 copy-start.2
  4.9 1.0 copy-start.3
  5.8 1.0 copy-start.4
  6.8 1.0 copy-start.5
  7.8 0.7 copy-start.6
  8.5 0.7 copy-start.7
  9.2 0.7 copy-start.8
  132.5 2.9 %copy-start.9 = (bf16[3,256,1536]{2,1,0:T(8,128)(2,1)S(1)}, bf16[3,256,1536]{2,1,0:T(8,128)(2,1)}, u32[]{:S(2)}) copy-start(bf16[3,256,1536]{2,1,0:T(8,128)(2,1)} %get-tuple-element.14) | copy-start | bytes 7077892

commit v2 on v1

--- a/solution.py
+++ b/solution.py
@@ -34,8 +34,8 @@
     vq, vk, vv, tq, tk, tv, qg, kg, gate, wt, go, tgo,
     o_video, o_text, o_w, o_gain,
     qb, kb, vb, dyr, dyb, wbuf, wslot, w48, dout, grads,
-    qn_s, kn_s, knt_s, vt_s, ot_s, dk_a, dv_a, gains,
-    tbuf, rbuf, zs, zr, xsum, xr, g_seq, g_x, g_y, g_z,
+    p_s, qn_s, kn_s, knt_s, vt_s, ot_s, dk_a, dv_a, gains,
+    tbuf, rbuf, zs, zr, xsum, xr, g_x, g_y, g_z,
     ssem, rsem, lsem,
 ):
     dp, s = lax.axis_index("dp"), lax.axis_index("seq")
@@ -43,7 +43,7 @@
     core = s + 1 - 2 * (s % 2)
     part = (s + 2) % NS
     diag = (core + 2) % NS
-    seq_peer = {1: core, 2: part, 3: diag}
+    seq_peer = {0: s, 1: core, 2: part, 3: diag}
 
     def ydev(k):
         return (xl * (NY * NZ) + ((y + NY + k) % NY) * NZ + z, s)
@@ -51,10 +51,14 @@
     def zdev(k):
         return (xl * (NY * NZ) + y * NZ + (z + NZ + k) % NZ, s)
 
-    xdev = ((dp + NY * NZ) % (XL * NY * NZ), s)
+    dpx = (dp + NY * NZ) % (XL * NY * NZ)
+    xdev = (dpx, s)
 
     def sdev(d):
         return (dp, seq_peer[d])
+
+    def xsdev(d):
+        return (dpx, seq_peer[d])
 
     names = {}
     pending = []
@@ -90,12 +94,13 @@
     def head_cols(j, h):
         return pl.ds(pl.multiple_of(j * GC + h * HD, HD), HD)
 
-    peers = [sdev(1), sdev(2), sdev(3), xdev] + [ydev(k) for k in range(1, NY)] + [zdev(k) for k in range(1, NZ)]
+    peers = [sdev(d) for d in (1, 2, 3)] + [xsdev(d) for d in range(NS)]
+    peers += [ydev(k) for k in range(1, NY)] + [zdev(k) for k in range(1, NZ)]
     barrier = pltpu.get_barrier_semaphore()
     for dev in peers:
         pl.semaphore_signal(barrier, inc=1, device_id=dev, device_id_type=MESH)
 
-    own_w = here(wt.at[:, cols_of(s)], wslot.at[s])
+    own_w = here(wt.at[:, cols_of(s)], wslot.at[xl, s])
     own_dy = here(go, dyr.at[rows_of(s)])
     text_dy = here(tgo, dyr.at[pl.ds(VID, TXT)])
     own = []
@@ -104,30 +109,41 @@
         own.append(here(tsrc.at[:, cols_of(s)], dst.at[pl.ds(VID, TXT)]))
     pl.semaphore_wait(barrier, len(peers))
 
-    for d in (1, 2, 3):
-        send(("w", d), wt.at[:, cols_of(seq_peer[d])], wslot.at[s], sdev(d))
+    for d in range(NS):
+        cols = wt.at[:, cols_of(seq_peer[d])]
+        if d:
+            send(("w", 0, d), cols, wslot.at[xl, s], sdev(d))
+        send(("w", 1, d), cols, wslot.at[xl, s], xsdev(d))
+
     piece = V // PIECES
 
     def dy_piece(j, t):
         return dyr.at[pl.ds(pl.multiple_of(j * V + t * piece, piece), piece)]
 
-    for t in range(PIECES):
-        send(("dyx", t), go.at[pl.ds(t * piece, piece)], dy_piece(s, t), sdev(2))
-    send("dyc", go, dyr.at[rows_of(s)], sdev(1))
-    for h in range(G):
+    def send_in(h):
         for d in (2, 3, 1):
             for n, (src, dst) in enumerate(((vq, qb), (vk, kb), (vv, vb))):
                 send(("in", h, d, n), src.at[:, head_cols(seq_peer[d], h)],
                      dst.at[rows_of(s), pl.ds(h * HD, HD)], sdev(d))
 
+    def wait_in(h):
+        for d in (2, 3, 1):
+            for n, dst in enumerate((qb, kb, vb)):
+                arrived(("in", h, d, n), dst.at[rows_of(seq_peer[d]), pl.ds(h * HD, HD)], sdev(d))
+
     own_w.wait()
-    for d in (1, 2, 3):
-        arrived(("w", d), wslot.at[seq_peer[d]], sdev(d))
-    for j in range(NS):
-        w48[pl.ds(j * WCOL, WCOL), :] = wslot[j].astype(F32)[:WCOL]
-    wbuf[xl, y, z] = w48[...].astype(BF)
-    send("wx", wbuf.at[xl, y, z], wbuf.at[xl, y, z], xdev)
-    arrived("wx", wbuf.at[1 - xl, y, z], xdev)
+    for d in range(NS):
+        if d:
+            arrived(("w", 0, d), wslot.at[xl, seq_peer[d]], sdev(d))
+        arrived(("w", 1, d), wslot.at[1 - xl, seq_peer[d]], xsdev(d))
+    for t in range(PIECES):
+        send(("dyx", t), go.at[pl.ds(t * piece, piece)], dy_piece(s, t), sdev(2))
+    send("dyc", go, dyr.at[rows_of(s)], sdev(1))
+    send_in(0)
+    for i in range(XL):
+        for j in range(NS):
+            w48[i, pl.ds(j * WCOL, WCOL), :] = wslot[i, j].astype(F32)[:WCOL]
+        wbuf[i, y, z] = w48[i].astype(BF)
 
     ca, cb = pl.ds(HD, GC - HD), pl.ds(0, HD)
 
@@ -183,7 +199,6 @@
             arrived(("wzb-", t), blk_b(1 + t), zdev(1))
             if t + 1 < last_m:
                 send(("wzb-", t + 1), blk_b(1 + t), blk_b(1 + t), zdev(-1))
-        pass_on_dy(t)
         if t == 0:
             own_dy.wait()
             gated(s, V)
@@ -193,22 +208,11 @@
         if t == 2:
             arrived("dyc", dyr.at[rows_of(core)], sdev(1))
             gated(core, V)
-    for t in range(last_p, PIECES):
+            send_in(1)
+    send_in(2)
+    for t in range(PIECES):
         pass_on_dy(t)
     gated(part, V)
-    for kz in range(NZ):
-        for k in range(1, NY):
-            arrived(("wya", kz, k), blk_a(-k, kz), ydev(-k))
-    for t in range(PIECES):
-        arrived(("dyr", t), dy_piece(diag, t), sdev(1))
-    gated(diag, V)
-
-    def dout_rows(i, carry):
-        at = pl.ds(pl.multiple_of(i * 128, 128), 128)
-        w = wbuf[...].reshape(D, GC)
-        dout[at, :] = dot(dyb[at, :], w).astype(BF)
-        return carry
-    lax.fori_loop(0, TOK // 128, dout_rows, 0)
 
     for copy in own:
         copy.wait()
@@ -221,31 +225,40 @@
     def through_norm(x, r, u):
         return r * u - x * (r * r * r) * (jnp.sum(u * x, axis=-1, keepdims=True) * (1.0 / HD))
 
-    def head(h):
+    def fwd(h):
         cols = pl.ds(h * HD, HD)
         qf = qb[:, cols].astype(F32)
-        qn_s[...] = (qf * norm(qf) * q_gain).astype(BF)
+        qn_s[h] = (qf * norm(qf) * q_gain).astype(BF)
         kf = kb[:, cols].astype(F32)
         kn = kf * norm(kf) * k_gain
-        kn_s[...] = kn.astype(BF)
-        knt_s[...] = kn.T.astype(BF)
+        kn_s[h] = kn.astype(BF)
+        knt_s[h] = kn.T.astype(BF)
         vt_s[...] = vb[:, cols].astype(F32).T.astype(BF)
+
+        def chunk(c, carry):
+            at = pl.ds(pl.multiple_of(c * QC, QC), QC)
+            e = jnp.exp2(dot(kn_s[h], qn_s[h, at, :], 1, 1) * (SCALE * LOG2E))
+            p = e * (1.0 / jnp.sum(e, axis=0, keepdims=True))
+            p_s[h, :, at] = p
+            ot_s[:, at] = dot(vt_s[...], p.astype(BF)).astype(BF)
+            return carry
+        lax.fori_loop(0, TOK // QC, chunk, 0)
+
+    def bwd(h):
+        cols = pl.ds(h * HD, HD)
         dk_a[...] = jnp.zeros_like(dk_a)
         dv_a[...] = jnp.zeros_like(dv_a)
 
         def chunk(c, carry):
             at = pl.ds(pl.multiple_of(c * QC, QC), QC)
-            qn, do = qn_s[at, :], dout[at, cols]
-            e = jnp.exp2(dot(kn_s[...], qn, 1, 1) * (SCALE * LOG2E))
-            p = e * (1.0 / jnp.sum(e, axis=0, keepdims=True))
-            pb = p.astype(BF)
-            dv_a[...] += dot(pb, do)
-            ot_s[:, at] = dot(vt_s[...], pb).astype(BF)
+            do = dout[at, cols]
+            p = p_s[h, :, at]
+            dv_a[...] += dot(p.astype(BF), do)
             dpr = dot(vb[:, cols], do, 1, 1)
             delta = jnp.sum(p * dpr, axis=0, keepdims=True)
             ds = (p * (dpr - delta)).astype(BF)
-            dk_a[...] += dot(ds, qn)
-            dqn = dot(knt_s[...], ds).T * SCALE
+            dk_a[...] += dot(ds, qn_s[h, at, :])
+            dqn = dot(knt_s[h], ds).T * SCALE
             x = qb[at, cols].astype(F32)
             r = norm(x)
             grads[h, 0, at, :] = through_norm(x, r, dqn * q_gain).astype(BF)
@@ -265,28 +278,52 @@
             tbuf[h, n // NY, n % NY] = dot(ot_s[...], dyb[:, at]).astype(BF)
             return carry
         lax.fori_loop(0, XL * NY, body, 0)
+        for k in range(1, NY):
+            send(("ty", h, k), tbuf.at[h, :, (y + k) % NY], rbuf.at[h, k - 1], ydev(k))
 
     text = pl.ds(VID, TXT)
     out_local = []
-    for h in range(G):
-        for d in (2, 3, 1):
-            for n, dst in enumerate((qb, kb, vb)):
-                arrived(("in", h, d, n), dst.at[rows_of(seq_peer[d]), pl.ds(h * HD, HD)], sdev(d))
-        head(h)
+
+    def send_out(h):
         to = head_cols(s, h)
         send(("text", h, 2), grads.at[h, :, text], o_text.at[:, :, to], sdev(2))
+        for d in (2, 3):
+            send(("out", h, d), grads.at[h, :, rows_of(seq_peer[d])], o_video.at[:, :, to], sdev(d))
         send(("text", h, 1), grads.at[h, :, text], o_text.at[:, :, to], sdev(1))
-        for d in (2, 3, 1):
-            send(("out", h, d), grads.at[h, :, rows_of(seq_peer[d])], o_video.at[:, :, to], sdev(d))
+        send(("out", h, 1), grads.at[h, :, rows_of(seq_peer[1])], o_video.at[:, :, to], sdev(1))
         out_local.append(here(grads.at[h, :, rows_of(s)], o_video.at[:, :, to]))
         out_local.append(here(grads.at[h, :, text], o_text.at[:, :, to]))
+
+    wait_in(0)
+    fwd(0)
+    for t in range(PIECES):
+        arrived(("dyr", t), dy_piece(diag, t), sdev(1))
+    gated(diag, V)
+    term(0)
+    for kz in range(NZ):
+        for k in range(1, NY):
+            arrived(("wya", kz, k), blk_a(-k, kz), ydev(-k))
+
+    def dout_rows(i, carry):
+        at = pl.ds(pl.multiple_of(i * 128, 128), 128)
+        w = wbuf[...].reshape(D, GC)
+        dout[at, :] = dot(dyb[at, :], w).astype(BF)
+        return carry
+    lax.fori_loop(0, TOK // 128, dout_rows, 0)
+
+    bwd(0)
+    send_out(0)
+    for h in (1, 2):
+        wait_in(h)
+        fwd(h)
         term(h)
-        for k in range(1, NY):
-            send(("ty", h, k), tbuf.at[h, :, (y + k) % NY], rbuf.at[h, k - 1], ydev(k))
-
-    g_seq[s] = gains[...]
-    for d in (1, 2, 3):
-        send(("gs", d), g_seq.at[s], g_seq.at[s], sdev(d))
+    for h in (1, 2):
+        bwd(h)
+        send_out(h)
+
+    g_y[y] = gains[...]
+    for k in range(1, NY):
+        send(("gy", k), g_y.at[y], g_y.at[y], ydev(k))
 
     def pass_on_text(h):
         at = o_text.at[:, :, head_cols(part, h)]
@@ -313,36 +350,40 @@
         xsum[:, :, h * HD:(h + 1) * HD] = total
 
     y_sum(0)
-    for d in (1, 2, 3):
-        arrived(("gs", d), g_seq.at[seq_peer[d]], sdev(d))
-    g_x[xl] = g_seq[0] + g_seq[1] + g_seq[2] + g_seq[3]
-    send("gx", g_x.at[xl], g_x.at[xl], xdev)
     pass_on_text(0)
-    y_sum(1)
-    arrived("gx", g_x.at[1 - xl], xdev)
-    g_y[y] = g_x[0] + g_x[1]
-    for k in range(1, NY):
-        send(("gy", k), g_y.at[y], g_y.at[y], ydev(k))
-    z_sum(0)
-    pass_on_text(1)
-    y_sum(2)
     for k in range(1, NY):
         arrived(("gy", k), g_y.at[(y + NY - k) % NY], ydev(-k))
     g_z[z] = (g_y[0] + g_y[1]) + (g_y[2] + g_y[3])
     for k in range(1, NZ):
         send(("gz", k), g_z.at[z], g_z.at[z], zdev(k))
+    y_sum(1)
+    pass_on_text(1)
+    y_sum(2)
+    z_sum(0)
     z_sum(1)
-    z_sum(2)
-    send("tx", xsum.at[1 - xl], xr, xdev)
     for k in range(1, NZ):
         arrived(("gz", k), g_z.at[(z + NZ - k) % NZ], zdev(-k))
     total = g_z[0]
     for k in range(1, NZ):
         total += g_z[k]
+    g_x[xl, s] = total
+    for d in range(NS):
+        if d:
+            send(("gx", 0, d), g_x.at[xl, s], g_x.at[xl, s], sdev(d))
+        send(("gx", 1, d), g_x.at[xl, s], g_x.at[xl, s], xsdev(d))
+    z_sum(2)
+    send("tx", xsum.at[1 - xl], xr, xdev)
+    pass_on_text(2)
+    for d in range(NS):
+        if d:
+            arrived(("gx", 0, d), g_x.at[xl, seq_peer[d]], sdev(d))
+        arrived(("gx", 1, d), g_x.at[1 - xl, seq_peer[d]], xsdev(d))
+    total = g_x[0, 0]
+    for j in range(1, XL * NS):
+        total += g_x[j // NS, j % NS]
     o_gain[...] = total
     arrived("tx", xr, xdev)
     o_w[...] = xsum[xl] + xr[...]
-    pass_on_text(2)
 
     for h in range(G):
         arrived(("text", h, 1), o_text.at[:, :, head_cols(core, h)], sdev(1))
@@ -376,13 +417,14 @@
             pltpu.VMEM((TOK, D), BF),
             pltpu.VMEM((TOK, D), BF),
             pltpu.VMEM((XL, NY, NZ, WB, GC), BF),
-            pltpu.VMEM((NS, 16, GC), BF),
-            pltpu.VMEM((WB, GC), F32),
+            pltpu.VMEM((XL, NS, 16, GC), BF),
+            pltpu.VMEM((XL, WB, GC), F32),
             pltpu.VMEM((TOK, GC), BF),
             pltpu.VMEM((G, 3, TOK, HD), BF),
-            pltpu.VMEM((TOK, HD), BF),
-            pltpu.VMEM((TOK, HD), BF),
-            pltpu.VMEM((HD, TOK), BF),
+            pltpu.VMEM((G, TOK, TOK), F32),
+            pltpu.VMEM((G, TOK, HD), BF),
+            pltpu.VMEM((G, TOK, HD), BF),
+            pltpu.VMEM((G, HD, TOK), BF),
             pltpu.VMEM((HD, TOK), BF),
             pltpu.VMEM((HD, TOK), BF),
             pltpu.VMEM((TOK, HD), F32),
@@ -394,8 +436,7 @@
             pltpu.VMEM((G, NZ - 1, XL, WB, HD), BF),
             pltpu.VMEM((XL, WB, GC), F32),
             pltpu.VMEM((WB, GC), F32),
-            pltpu.VMEM((NS, 8, HD), F32),
-            pltpu.VMEM((XL, 8, HD), F32),
+            pltpu.VMEM((XL, NS, 8, HD), F32),
             pltpu.VMEM((NY, 8, HD), F32),
             pltpu.VMEM((NZ, 8, HD), F32),
             pltpu.SemaphoreType.DMA((160,)),
@@ -403,7 +444,7 @@
             pltpu.SemaphoreType.DMA((16,)),
         ],
         compiler_params=pltpu.CompilerParams(
-            collective_id=0, has_side_effects=True, vmem_limit_bytes=50 << 20
+            collective_id=0, has_side_effects=True, vmem_limit_bytes=62 << 20
         ),
         cost_estimate=pl.CostEstimate(flops=7 * 10**9, bytes_accessed=14 << 20, transcendentals=1 << 21),
     )(

time: 138 us -> 99.7 us (0.72)
  Pallas kernels: 123 us -> 91.5 us
  local copies, waits for them, and re-layouts: 14.2 us -> 7.2 us
    pallas_call x1, Pallas kernels: 123 us -> 91.5 us  [shards(): pl.pallas_call(kernel, out_shape=[jax.ShapeDtypeStruct((3, V, NS * GC), B...]
    unnamed x21 -> x5, local copies, waits for them, and re-layouts: 9.03 us -> 0.64 us
where the time goes in v2:
time: 99.7 us; the launch traced here: 99.4 us
  Pallas kernels  91.5 us (92%)
  local copies, waits for them, and re-layouts  7.2 us (7%)
    pallas_call x1, Pallas kernels, shards(): pl.pallas_call(kernel, out_shape=[jax.ShapeDtypeStruct((3, V, NS * GC), B...  91.5 us
    squeeze x1, local copies, waits for them, and re-layouts, shards(): video[2]  2.41 us

profile of v2, /device:TPU:1, one launch (start us, length us, event | category | flops | bytes accessed | tf_op | source)
XLA Modules:
  0.0 99.4 jit_solution(15605127616565092097)
XLA Ops:
  0.6 1.4 %pad.4.wt = bf16[16,1536]{1,0:T(8,128)(2,1)} pad(bf16[12,1536]{1,0:T(8,128)(2,1)} %bitcast.21, bf16[]{:T(256)} %constant.2.clone.1), padding=0_4x0_0 | pad | bytes 86018 | tf_op jit(solution)/shard_map/jit(_pad)/pad | solution.py:400
  2.1 91.5 %shard_map.187 = (bf16[3,128,1536]{2,1,0:T(8,128)(2,1)}, bf16[3,256,1536]{2,1,0:T(8,128)(2,1)}, f32[48,384]{1,0:T(8,128)}, f32[8,128]{1,0:T(8,128)}) custom-call(bf16[128,1536]{1,0:T(8,128)(2,1)} %vq.1, bf16[128,1536]{1,0:T(8,128)(2,1)} %vk.1, bf16[128,1536]{1,0:T(8,128)(2,1)} %vv.1, bf16[256,1536]{1,0:T(8,128)(2,1)} %tq.1, bf16[256,1536]{1,0:T(8,128)(2,1)} %tk.1, ...), custom_call_target="tpu_custom_call" | custom-call | flops 7000000000 | bytes 14680064 | tf_op jit(solution)/shard_map/pallas_call | solution.py:403
  93.6 0.0 copy-start
  93.6 2.4 %slice_bitcast_fusion.3 = (bf16[128,1536]{1,0:T(8,128)(2,1)}, bf16[128,1536]{1,0:T(8,128)(2,1)}, bf16[128,1536]{1,0:T(8,128)(2,1)}) fusion(bf16[3,128,1536]{2,1,0:T(8,128)(2,1)} %get-tuple-element.13), kind=kLoop, calls=%fused_computation.3 | loop fusion | bytes 2359296 | tf_op jit(solution)/shard_map/squeeze | solution.py:455
  96.0 1.3 %slice_bitcast_fusion.6 = (f32[128]{0:T(128)}, f32[128]{0:T(128)}) fusion(f32[8,128]{1,0:T(8,128)} %get-tuple-element.16), kind=kLoop, calls=%fused_computation.6 | loop fusion | bytes 2048 | tf_op jit(solution)/shard_map/squeeze | solution.py:456
  97.3 0.0 copy-done
  97.3 0.0 copy-start.1
  97.3 1.4 %slice_bitcast_fusion = (bf16[256,1536]{1,0:T(8,128)(2,1)}, bf16[256,1536]{1,0:T(8,128)(2,1)}, bf16[256,1536]{1,0:T(8,128)(2,1)}) fusion(bf16[3,256,1536]{2,1,0:T(8,128)(2,1)S(1)} %copy-done), kind=kLoop, calls=%fused_computation | loop fusion | bytes 4718592 | tf_op jit(solution)/shard_map/squeeze | solution.py:455
  98.7 0.0 copy-done.1
  98.7 0.6 copy.22
Async XLA Ops:
  93.6 3.7 %copy-start = (bf16[3,256,1536]{2,1,0:T(8,128)(2,1)S(1)}, bf16[3,256,1536]{2,1,0:T(8,128)(2,1)}, u32[]{:S(2)}) copy-start(bf16[3,256,1536]{2,1,0:T(8,128)(2,1)} %get-tuple-element.14) | copy-start | bytes 7077892
  97.3 1.5 %copy-start.1 = (f32[48,384]{1,0:T(8,128)S(1)}, f32[48,384]{1,0:T(8,128)}, u32[]{:S(2)}) copy-start(f32[48,384]{1,0:T(8,128)} %get-tuple-element.15) | copy-start | bytes 221188

commit v3 on v2

--- a/solution.py
+++ b/solution.py
@@ -20,8 +20,9 @@
 D = 3072
 WCOL = 12
 WB = 48
-QC = 256
+QC = 768
 PIECES = 8
+SEMS = 192
 SCALE = HD**-0.5
 LOG2E = 1.4426950408889634
 
@@ -35,7 +36,7 @@
     o_video, o_text, o_w, o_gain,
     qb, kb, vb, dyr, dyb, wbuf, wslot, w48, dout, grads,
     p_s, qn_s, kn_s, knt_s, vt_s, ot_s, dk_a, dv_a, gains,
-    tbuf, rbuf, zs, zr, xsum, xr, g_x, g_y, g_z,
+    tbuf, r1, rbuf, zs, zr, xsum, xr, g_x, g_y, g_z,
     ssem, rsem, lsem,
 ):
     dp, s = lax.axis_index("dp"), lax.axis_index("seq")
@@ -66,6 +67,7 @@
 
     def remote(key, src, dst, dev):
         i = names.setdefault(key, len(names))
+        assert i < SEMS
         return pltpu.make_async_remote_copy(
             src_ref=src, dst_ref=dst, send_sem=ssem.at[i], recv_sem=rsem.at[i],
             device_id=dev, device_id_type=MESH,
@@ -272,14 +274,28 @@
         gains[1:2, :] += jnp.sum(dkn * x * r, axis=0, keepdims=True)
         grads[h, 2] = dv_a[...].astype(BF)
 
+    lo, hi = pl.ds(0, HD // 2), pl.ds(HD // 2, HD // 2)
+
     def term(h):
-        def body(n, carry):
-            at = pl.ds(pl.multiple_of(n * GC, GC), GC)
-            tbuf[h, n // NY, n % NY] = dot(ot_s[...], dyb[:, at]).astype(BF)
+        def body(i, carry):
+            at = pl.ds(pl.multiple_of(i * NY * GC, NY * GC), NY * GC)
+            t = dot(ot_s[...], dyb[:, at]).astype(BF)
+            for j in range(NY):
+                tbuf[h, i, j] = t[:, j * GC:(j + 1) * GC]
             return carry
-        lax.fori_loop(0, XL * NY, body, 0)
-        for k in range(1, NY):
-            send(("ty", h, k), tbuf.at[h, :, (y + k) % NY], rbuf.at[h, k - 1], ydev(k))
+        lax.fori_loop(0, XL, body, 0)
+        far = tbuf.at[h, :, (y + 2) % NY]
+        send(("ty+", h), far.at[:, lo], r1.at[h, 0], ydev(1))
+        send(("ty-", h), far.at[:, hi], r1.at[h, 1], ydev(-1))
+
+    def y_mid(h):
+        for i, half, k, key in ((0, lo, 1, "+"), (1, hi, -1, "-")):
+            arrived(("ty" + key, h), r1.at[h, i], ydev(-k))
+            to = (y + NY + k) % NY
+            for j in range(XL):
+                both = tbuf[h, j, to, half].astype(F32) + r1[h, i, j].astype(F32)
+                tbuf[h, j, to, half] = both.astype(BF)
+            send(("tyy" + key, h), tbuf.at[h, :, to], rbuf.at[h, i], ydev(k))
 
     text = pl.ds(VID, TXT)
     out_local = []
@@ -294,6 +310,15 @@
         out_local.append(here(grads.at[h, :, rows_of(s)], o_video.at[:, :, to]))
         out_local.append(here(grads.at[h, :, text], o_text.at[:, :, to]))
 
+    def y_sum(h):
+        arrived(("tyy+", h), rbuf.at[h, 0], ydev(-1))
+        arrived(("tyy-", h), rbuf.at[h, 1], ydev(1))
+        for i in range(XL):
+            total = tbuf[h, i, y].astype(F32) + rbuf[h, 0, i].astype(F32) + rbuf[h, 1, i].astype(F32)
+            zs[h, :, i] = total.T.reshape(NZ, WB, HD).astype(BF)
+        for k in range(1, NZ):
+            send(("tz", h, k), zs.at[h, (z + k) % NZ], zr.at[h, k - 1], zdev(k))
+
     wait_in(0)
     fwd(0)
     for t in range(PIECES):
@@ -304,22 +329,23 @@
         for k in range(1, NY):
             arrived(("wya", kz, k), blk_a(-k, kz), ydev(-k))
 
-    def dout_rows(i, carry):
-        at = pl.ds(pl.multiple_of(i * 128, 128), 128)
-        w = wbuf[...].reshape(D, GC)
-        dout[at, :] = dot(dyb[at, :], w).astype(BF)
-        return carry
-    lax.fori_loop(0, TOK // 128, dout_rows, 0)
-
+    dout[...] = dot(dyb[...], wbuf[...].reshape(D, GC)).astype(BF)
+
+    y_mid(0)
     bwd(0)
     send_out(0)
-    for h in (1, 2):
-        wait_in(h)
-        fwd(h)
-        term(h)
-    for h in (1, 2):
-        bwd(h)
-        send_out(h)
+    wait_in(1)
+    fwd(1)
+    term(1)
+    wait_in(2)
+    fwd(2)
+    term(2)
+    bwd(1)
+    send_out(1)
+    y_mid(1)
+    y_sum(0)
+    bwd(2)
+    send_out(2)
 
     g_y[y] = gains[...]
     for k in range(1, NY):
@@ -329,17 +355,6 @@
         at = o_text.at[:, :, head_cols(part, h)]
         arrived(("text", h, 2), at, sdev(2))
         send(("textr", h), at, at, sdev(1))
-
-    def y_sum(h):
-        for k in range(1, NY):
-            arrived(("ty", h, k), rbuf.at[h, k - 1], ydev(-k))
-        for i in range(XL):
-            total = tbuf[h, i, y].astype(F32)
-            for k in range(1, NY):
-                total += rbuf[h, k - 1, i].astype(F32)
-            zs[h, :, i] = total.T.reshape(NZ, WB, HD).astype(BF)
-        for k in range(1, NZ):
-            send(("tz", h, k), zs.at[h, (z + k) % NZ], zr.at[h, k - 1], zdev(k))
 
     def z_sum(h):
         for k in range(1, NZ):
@@ -349,16 +364,14 @@
             total += zr[h, k - 1].astype(F32)
         xsum[:, :, h * HD:(h + 1) * HD] = total
 
-    y_sum(0)
-    pass_on_text(0)
+    y_mid(2)
+    y_sum(1)
+    y_sum(2)
     for k in range(1, NY):
         arrived(("gy", k), g_y.at[(y + NY - k) % NY], ydev(-k))
     g_z[z] = (g_y[0] + g_y[1]) + (g_y[2] + g_y[3])
     for k in range(1, NZ):
         send(("gz", k), g_z.at[z], g_z.at[z], zdev(k))
-    y_sum(1)
-    pass_on_text(1)
-    y_sum(2)
     z_sum(0)
     z_sum(1)
     for k in range(1, NZ):
@@ -373,7 +386,8 @@
         send(("gx", 1, d), g_x.at[xl, s], g_x.at[xl, s], xsdev(d))
     z_sum(2)
     send("tx", xsum.at[1 - xl], xr, xdev)
-    pass_on_text(2)
+    for h in range(G):
+        pass_on_text(h)
     for d in range(NS):
         if d:
             arrived(("gx", 0, d), g_x.at[xl, seq_peer[d]], sdev(d))
@@ -431,7 +445,8 @@
             pltpu.VMEM((TOK, HD), F32),
             pltpu.VMEM((8, HD), F32),
             pltpu.VMEM((G, XL, NY, HD, GC), BF),
-            pltpu.VMEM((G, NY - 1, XL, HD, GC), BF),
+            pltpu.VMEM((G, 2, XL, HD // 2, GC), BF),
+            pltpu.VMEM((G, 2, XL, HD, GC), BF),
             pltpu.VMEM((G, NZ, XL, WB, HD), BF),
             pltpu.VMEM((G, NZ - 1, XL, WB, HD), BF),
             pltpu.VMEM((XL, WB, GC), F32),
@@ -439,8 +454,8 @@
             pltpu.VMEM((XL, NS, 8, HD), F32),
             pltpu.VMEM((NY, 8, HD), F32),
             pltpu.VMEM((NZ, 8, HD), F32),
-            pltpu.SemaphoreType.DMA((160,)),
-            pltpu.SemaphoreType.DMA((160,)),
+            pltpu.SemaphoreType.DMA((SEMS,)),
+            pltpu.SemaphoreType.DMA((SEMS,)),
             pltpu.SemaphoreType.DMA((16,)),
         ],
         compiler_params=pltpu.CompilerParams(

time: 99.7 us -> 89.7 us (0.90)
  Pallas kernels: 91.5 us -> 81.6 us
    pallas_call x1, Pallas kernels: 91.5 us -> 81.6 us  [shards(): pl.pallas_call(kernel, out_shape=[jax.ShapeDtypeStruct((3, V, NS * GC), B...]
where the time goes in v3:
time: 89.7 us; the launch traced here: 89.4 us
  Pallas kernels  81.6 us (91%)
  local copies, waits for them, and re-layouts  7.2 us (8%)
    pallas_call x1, Pallas kernels, shards(): pl.pallas_call(kernel, out_shape=[jax.ShapeDtypeStruct((3, V, NS * GC), B...  81.6 us
    squeeze x1, local copies, waits for them, and re-layouts, shards(): video[2]  2.41 us

profile of v3, /device:TPU:1, one launch (start us, length us, event | category | flops | bytes accessed | tf_op | source)
XLA Modules:
  0.0 89.4 jit_solution(13846442646302219962)
XLA Ops:
  0.6 1.4 %pad.4.wt = bf16[16,1536]{1,0:T(8,128)(2,1)} pad(bf16[12,1536]{1,0:T(8,128)(2,1)} %bitcast.21, bf16[]{:T(256)} %constant.2.clone.1), padding=0_4x0_0 | pad | bytes 86018 | tf_op jit(solution)/shard_map/jit(_pad)/pad | solution.py:414
  2.1 81.6 %shard_map.187 = (bf16[3,128,1536]{2,1,0:T(8,128)(2,1)}, bf16[3,256,1536]{2,1,0:T(8,128)(2,1)}, f32[48,384]{1,0:T(8,128)}, f32[8,128]{1,0:T(8,128)}) custom-call(bf16[128,1536]{1,0:T(8,128)(2,1)} %vq.1, bf16[128,1536]{1,0:T(8,128)(2,1)} %vk.1, bf16[128,1536]{1,0:T(8,128)(2,1)} %vv.1, bf16[256,1536]{1,0:T(8,128)(2,1)} %tq.1, bf16[256,1536]{1,0:T(8,128)(2,1)} %tk.1, ...), custom_call_target="tpu_custom_call" | custom-call | flops 7000000000 | bytes 14680064 | tf_op jit(solution)/shard_map/pallas_call | solution.py:417
  83.7 0.0 copy-start
  83.7 2.4 %slice_bitcast_fusion.3 = (bf16[128,1536]{1,0:T(8,128)(2,1)}, bf16[128,1536]{1,0:T(8,128)(2,1)}, bf16[128,1536]{1,0:T(8,128)(2,1)}) fusion(bf16[3,128,1536]{2,1,0:T(8,128)(2,1)} %get-tuple-element.13), kind=kLoop, calls=%fused_computation.3 | loop fusion | bytes 2359296 | tf_op jit(solution)/shard_map/squeeze | solution.py:470
  86.1 1.3 %slice_bitcast_fusion.6 = (f32[128]{0:T(128)}, f32[128]{0:T(128)}) fusion(f32[8,128]{1,0:T(8,128)} %get-tuple-element.16), kind=kLoop, calls=%fused_computation.6 | loop fusion | bytes 2048 | tf_op jit(solution)/shard_map/squeeze | solution.py:471
  87.3 0.0 copy-done
  87.4 0.0 copy-start.1
  87.4 1.4 %slice_bitcast_fusion = (bf16[256,1536]{1,0:T(8,128)(2,1)}, bf16[256,1536]{1,0:T(8,128)(2,1)}, bf16[256,1536]{1,0:T(8,128)(2,1)}) fusion(bf16[3,256,1536]{2,1,0:T(8,128)(2,1)S(1)} %copy-done), kind=kLoop, calls=%fused_computation | loop fusion | bytes 4718592 | tf_op jit(solution)/shard_map/squeeze | solution.py:470
  88.8 0.0 copy-done.1
  88.8 0.6 copy.22
Async XLA Ops:
  83.7 3.7 %copy-start = (bf16[3,256,1536]{2,1,0:T(8,128)(2,1)S(1)}, bf16[3,256,1536]{2,1,0:T(8,128)(2,1)}, u32[]{:S(2)}) copy-start(bf16[3,256,1536]{2,1,0:T(8,128)(2,1)} %get-tuple-element.14) | copy-start | bytes 7077892
  87.4 1.5 %copy-start.1 = (f32[48,384]{1,0:T(8,128)S(1)}, f32[48,384]{1,0:T(8,128)}, u32[]{:S(2)}) copy-start(f32[48,384]{1,0:T(8,128)} %get-tuple-element.15) | copy-start | bytes 221188

commit v4 on v3

--- a/solution.py
+++ b/solution.py
@@ -23,6 +23,7 @@
 QC = 768
 PIECES = 8
 SEMS = 192
+EARLY = 4
 SCALE = HD**-0.5
 LOG2E = 1.4426950408889634
 
@@ -32,9 +33,9 @@
 
 
 def kernel(
-    vq, vk, vv, tq, tk, tv, qg, kg, gate, wt, go, tgo,
+    vq, vk, vv, tq, tk, tv, qg, kg, gate, w_own, go, tgo,
     o_video, o_text, o_w, o_gain,
-    qb, kb, vb, dyr, dyb, wbuf, wslot, w48, dout, grads,
+    wt, qb, kb, vb, dyr, dyb, wbuf, wslot, w48, dout, grads,
     p_s, qn_s, kn_s, knt_s, vt_s, ot_s, dk_a, dv_a, gains,
     tbuf, r1, rbuf, zs, zr, xsum, xr, g_x, g_y, g_z,
     ssem, rsem, lsem,
@@ -102,6 +103,8 @@
     for dev in peers:
         pl.semaphore_signal(barrier, inc=1, device_id=dev, device_id_type=MESH)
 
+    wt[...] = jnp.zeros_like(wt)
+    wt[pl.ds(0, WCOL), :] = w_own[...]
     own_w = here(wt.at[:, cols_of(s)], wslot.at[xl, s])
     own_dy = here(go, dyr.at[rows_of(s)])
     text_dy = here(tgo, dyr.at[pl.ds(VID, TXT)])
@@ -122,6 +125,9 @@
     def dy_piece(j, t):
         return dyr.at[pl.ds(pl.multiple_of(j * V + t * piece, piece), piece)]
 
+    for t in range(EARLY):
+        send(("dyx", t), go.at[pl.ds(t * piece, piece)], dy_piece(s, t), sdev(2))
+
     def send_in(h):
         for d in (2, 3, 1):
             for n, (src, dst) in enumerate(((vq, qb), (vk, kb), (vv, vb))):
@@ -138,7 +144,7 @@
         if d:
             arrived(("w", 0, d), wslot.at[xl, seq_peer[d]], sdev(d))
         arrived(("w", 1, d), wslot.at[1 - xl, seq_peer[d]], xsdev(d))
-    for t in range(PIECES):
+    for t in range(EARLY, PIECES):
         send(("dyx", t), go.at[pl.ds(t * piece, piece)], dy_piece(s, t), sdev(2))
     send("dyc", go, dyr.at[rows_of(s)], sdev(1))
     send_in(0)
@@ -331,9 +337,9 @@
 
     dout[...] = dot(dyb[...], wbuf[...].reshape(D, GC)).astype(BF)
 
-    y_mid(0)
     bwd(0)
     send_out(0)
+    y_mid(0)
     wait_in(1)
     fwd(1)
     term(1)
@@ -365,6 +371,7 @@
         xsum[:, :, h * HD:(h + 1) * HD] = total
 
     y_mid(2)
+    pass_on_text(0)
     y_sum(1)
     y_sum(2)
     for k in range(1, NY):
@@ -372,6 +379,7 @@
     g_z[z] = (g_y[0] + g_y[1]) + (g_y[2] + g_y[3])
     for k in range(1, NZ):
         send(("gz", k), g_z.at[z], g_z.at[z], zdev(k))
+    pass_on_text(1)
     z_sum(0)
     z_sum(1)
     for k in range(1, NZ):
@@ -386,8 +394,7 @@
         send(("gx", 1, d), g_x.at[xl, s], g_x.at[xl, s], xsdev(d))
     z_sum(2)
     send("tx", xsum.at[1 - xl], xr, xdev)
-    for h in range(G):
-        pass_on_text(h)
+    pass_on_text(2)
     for d in range(NS):
         if d:
             arrived(("gx", 0, d), g_x.at[xl, seq_peer[d]], sdev(d))
@@ -410,9 +417,21 @@
         copy.wait_send()
 
 
+def place(video, text, w, gains, *rest):
+    outs, (row_q, row_k, sems) = rest[:9], rest[9:]
+    row_q[...] = gains[0:1, :]
+    row_k[...] = gains[1:2, :]
+    parts = [(text.at[n], outs[3 + n]) for n in range(3)] + [(video.at[n], outs[n]) for n in range(3)]
+    parts += [(w, outs[6]), (row_q, outs[7]), (row_k, outs[8])]
+    copies = [pltpu.make_async_copy(src, dst, sems.at[n]) for n, (src, dst) in enumerate(parts)]
+    for copy in copies:
+        copy.start()
+    for copy in copies:
+        copy.wait()
+
+
 def shards(video_q, video_k, video_v, text_q, text_k, text_v, q_gain, k_gain, gate, out_weight, grad_out, text_grad_out):
-    wt = jnp.pad(out_weight.T, ((0, 16 - WCOL), (0, 0)))
-    hbm = pl.BlockSpec(memory_space=pl.ANY)
+    hbm = pl.BlockSpec(memory_space=pltpu.HBM)
     vmem = pl.BlockSpec(memory_space=pltpu.VMEM)
     video, text, w, gains = pl.pallas_call(
         kernel,
@@ -422,9 +441,10 @@
             jax.ShapeDtypeStruct((WB, GC), F32),
             jax.ShapeDtypeStruct((8, HD), F32),
         ],
-        in_specs=[hbm] * 6 + [vmem] * 3 + [hbm] * 3,
-        out_specs=[hbm, hbm, vmem, vmem],
+        in_specs=[hbm] * 6 + [vmem] * 4 + [hbm] * 2,
+        out_specs=[vmem] * 4,
         scratch_shapes=[
+            pltpu.VMEM((16, NS * GC), BF),
             pltpu.VMEM((TOK, GC), BF),
             pltpu.VMEM((TOK, GC), BF),
             pltpu.VMEM((TOK, GC), BF),
@@ -459,17 +479,23 @@
             pltpu.SemaphoreType.DMA((16,)),
         ],
         compiler_params=pltpu.CompilerParams(
-            collective_id=0, has_side_effects=True, vmem_limit_bytes=62 << 20
+            collective_id=0, has_side_effects=True, vmem_limit_bytes=54 << 20
         ),
         cost_estimate=pl.CostEstimate(flops=7 * 10**9, bytes_accessed=14 << 20, transcendentals=1 << 21),
     )(
         video_q, video_k, video_v, text_q, text_k, text_v,
-        q_gain.reshape(1, HD), k_gain.reshape(1, HD), gate, wt, grad_out, text_grad_out,
+        q_gain.reshape(1, HD), k_gain.reshape(1, HD), gate, out_weight.T, grad_out, text_grad_out,
     )
-    return (
-        video[0], video[1], video[2], text[0], text[1], text[2],
-        w.T, gains[0], gains[1],
-    )
+    rows = [jax.ShapeDtypeStruct((V, NS * GC), BF)] * 3 + [jax.ShapeDtypeStruct((TXT, NS * GC), BF)] * 3
+    outs = pl.pallas_call(
+        place,
+        out_shape=rows + [jax.ShapeDtypeStruct((WB, GC), F32)] + [jax.ShapeDtypeStruct((1, HD), F32)] * 2,
+        in_specs=[vmem] * 4,
+        out_specs=[hbm] * 9,
+        scratch_shapes=[pltpu.VMEM((1, HD), F32), pltpu.VMEM((1, HD), F32), pltpu.SemaphoreType.DMA((9,))],
+        cost_estimate=pl.CostEstimate(flops=0, bytes_accessed=7 << 20, transcendentals=0),
+    )(video, text, w, gains)
+    return (*outs[:6], outs[6].T, outs[7].reshape(HD), outs[8].reshape(HD))
 
 
 def solution(mesh):

time: 89.7 us -> 85.3 us (0.951)
  local copies, waits for them, and re-layouts: 7.2 us -> 0 us
  Pallas kernels: 81.6 us -> 84.3 us
    squeeze x3 -> x0, local copies, waits for them, and re-layouts: 5.13 us -> none  [the longest x1 2.41 us: shards(): video[2]]
    pallas_call x0 -> x1, Pallas kernels: none -> 3.87 us  [shards(): pl.pallas_call(place, out_shape=rows + [jax.ShapeDtypeStruct((WB, GC), F3...]
    pad x1 -> x0, local copies, waits for them, and re-layouts: 1.43 us -> none  [shards(): wt = jnp.pad(out_weight.T, ((0, 16 - WCOL), (0, 0)))]
    pallas_call x1, Pallas kernels: 81.6 us -> 80.5 us  [shards(): pl.pallas_call(kernel, out_shape=[jax.ShapeDtypeStruct((3, V, NS * GC), B...]
where the time goes in v4:
time: 85.3 us; the launch traced here: 85.1 us
  Pallas kernels  84.3 us (99%)
    pallas_call x1, Pallas kernels, shards(): pl.pallas_call(kernel, out_shape=[jax.ShapeDtypeStruct((3, V, NS * GC), B...  80.5 us
    pallas_call x1, Pallas kernels, shards(): pl.pallas_call(place, out_shape=rows + [jax.ShapeDtypeStruct((WB, GC), F3...  3.87 us

profile of v4, /device:TPU:1, one launch (start us, length us, event | category | flops | bytes accessed | tf_op | source)
XLA Modules:
  0.0 85.1 jit_solution(6710309100382856645)
XLA Ops:
  0.6 80.5 %shard_map.187 = (bf16[3,128,1536]{2,1,0:T(8,128)(2,1)}, bf16[3,256,1536]{2,1,0:T(8,128)(2,1)}, f32[48,384]{1,0:T(8,128)}, f32[8,128]{1,0:T(8,128)}) custom-call(bf16[128,1536]{1,0:T(8,128)(2,1)} %vq.1, bf16[128,1536]{1,0:T(8,128)(2,1)} %vk.1, bf16[128,1536]{1,0:T(8,128)(2,1)} %vv.1, bf16[256,1536]{1,0:T(8,128)(2,1)} %tq.1, bf16[256,1536]{1,0:T(8,128)(2,1)} %tk.1, ...), custom_call_target="tpu_custom_call" | custom-call | flops 7000000000 | bytes 14680064 | tf_op jit(solution)/shard_map/pallas_call | solution.py:436
  81.1 3.9 %shard_map.188 = (bf16[128,1536]{1,0:T(8,128)(2,1)}, bf16[128,1536]{1,0:T(8,128)(2,1)}, bf16[128,1536]{1,0:T(8,128)(2,1)}, bf16[256,1536]{1,0:T(8,128)(2,1)}, bf...) custom-call(bf16[3,128,1536]{2,1,0:T(8,128)(2,1)} %get-tuple-element, ...), custom_call_target="tpu_custom_call" | custom-call | bytes 7340032 | tf_op jit(solution)/shard_map/pallas_call | solution.py:490

commit v5 on v4

--- a/solution.py
+++ b/solution.py
@@ -368,20 +368,22 @@
         total = zs[h, z].astype(F32)
         for k in range(1, NZ):
             total += zr[h, k - 1].astype(F32)
-        xsum[:, :, h * HD:(h + 1) * HD] = total
+        cols = pl.ds(h * HD, HD)
+        xsum[:, :, cols] = total
+        send(("tx", h), xsum.at[1 - xl, :, cols], xr.at[:, cols], xdev)
 
     y_mid(2)
-    pass_on_text(0)
     y_sum(1)
-    y_sum(2)
     for k in range(1, NY):
         arrived(("gy", k), g_y.at[(y + NY - k) % NY], ydev(-k))
     g_z[z] = (g_y[0] + g_y[1]) + (g_y[2] + g_y[3])
     for k in range(1, NZ):
         send(("gz", k), g_z.at[z], g_z.at[z], zdev(k))
+    z_sum(0)
+    pass_on_text(0)
+    y_sum(2)
+    z_sum(1)
     pass_on_text(1)
-    z_sum(0)
-    z_sum(1)
     for k in range(1, NZ):
         arrived(("gz", k), g_z.at[(z + NZ - k) % NZ], zdev(-k))
     total = g_z[0]
@@ -393,7 +395,6 @@
             send(("gx", 0, d), g_x.at[xl, s], g_x.at[xl, s], sdev(d))
         send(("gx", 1, d), g_x.at[xl, s], g_x.at[xl, s], xsdev(d))
     z_sum(2)
-    send("tx", xsum.at[1 - xl], xr, xdev)
     pass_on_text(2)
     for d in range(NS):
         if d:
@@ -403,7 +404,8 @@
     for j in range(1, XL * NS):
         total += g_x[j // NS, j % NS]
     o_gain[...] = total
-    arrived("tx", xr, xdev)
+    for h in range(G):
+        arrived(("tx", h), xr.at[:, pl.ds(h * HD, HD)], xdev)
     o_w[...] = xsum[xl] + xr[...]
 
     for h in range(G):

time: 85.3 us -> 83.3 us (0.977)
  Pallas kernels: 84.3 us -> 82.4 us
    pallas_call x1, Pallas kernels: 80.5 us -> 78.5 us  [shards(): pl.pallas_call(kernel, out_shape=[jax.ShapeDtypeStruct((3, V, NS * GC), B...]
where the time goes in v5:
time: 83.3 us; the launch traced here: 83.2 us
  Pallas kernels  82.4 us (99%)
    pallas_call x1, Pallas kernels, shards(): pl.pallas_call(kernel, out_shape=[jax.ShapeDtypeStruct((3, V, NS * GC), B...  78.5 us
    pallas_call x1, Pallas kernels, shards(): pl.pallas_call(place, out_shape=rows + [jax.ShapeDtypeStruct((WB, GC), F3...  3.87 us

profile of v5, /device:TPU:1, one launch (start us, length us, event | category | flops | bytes accessed | tf_op | source)
XLA Modules:
  0.0 83.2 jit_solution(11539937888111436757)
XLA Ops:
  0.6 78.5 %shard_map.187 = (bf16[3,128,1536]{2,1,0:T(8,128)(2,1)}, bf16[3,256,1536]{2,1,0:T(8,128)(2,1)}, f32[48,384]{1,0:T(8,128)}, f32[8,128]{1,0:T(8,128)}) custom-call(bf16[128,1536]{1,0:T(8,128)(2,1)} %vq.1, bf16[128,1536]{1,0:T(8,128)(2,1)} %vk.1, bf16[128,1536]{1,0:T(8,128)(2,1)} %vv.1, bf16[256,1536]{1,0:T(8,128)(2,1)} %tq.1, bf16[256,1536]{1,0:T(8,128)(2,1)} %tk.1, ...), custom_call_target="tpu_custom_call" | custom-call | flops 7000000000 | bytes 14680064 | tf_op jit(solution)/shard_map/pallas_call | solution.py:438
  79.1 3.9 %shard_map.188 = (bf16[128,1536]{1,0:T(8,128)(2,1)}, bf16[128,1536]{1,0:T(8,128)(2,1)}, bf16[128,1536]{1,0:T(8,128)(2,1)}, bf16[256,1536]{1,0:T(8,128)(2,1)}, bf...) custom-call(bf16[3,128,1536]{2,1,0:T(8,128)(2,1)} %get-tuple-element, ...), custom_call_target="tpu_custom_call" | custom-call | bytes 7340032 | tf_op jit(solution)/shard_map/pallas_call | solution.py:492
